TPU v7x, 256 devices: a whole 4x4x8 slice. The times are simulated.
256 devices in a mesh: row: 4 (over y), col: 8 (over z), depth: 8 (over x, core).
Axes of the slice: x: 4, y: 4, z: 8, core: 2. Of those that a mesh axis runs over, the one named last changes fastest.
Arguments:
- inputs: bfloat16 [512, 12288], P(('row', 'depth'), 'col'), may hold values from -6 to 6
- w_in: bfloat16 [12288, 24576], P('col', ('row', 'depth')), may hold values from -0.0546875 to 0.0546875
- w_out: bfloat16 [24576, 12288], P(('row', 'depth'), 'col'), may hold values from -0.0390625 to 0.0390625
- grad_out: bfloat16 [512, 12288], P(('row', 'depth'), 'col'), may hold values from -6 to 6
Outputs:
- outputs: bfloat16 [512, 12288], P(('row', 'depth'), 'col')
- grad_in: bfloat16 [512, 12288], P(('row', 'depth'), 'col')
- grad_w_in: bfloat16 [12288, 24576], P('col', ('row', 'depth'))
- grad_w_out: bfloat16 [24576, 12288], P(('row', 'depth'), 'col')
All inputs are finite; a program needn't handle non-finite values.
Results may differ from a plain program's by a relative error of at most 0.005.
Values may be sent and summed in bfloat16 or wider, within the bound.
A program may use at most 64 MiB of HBM per device.

v0:
```python
import jax
import jax.numpy as jnp
from jax import lax
from jax.sharding import PartitionSpec as P


def gelu_parts(hidden):
    inner = 0.7978845608 * (hidden + 0.044715 * hidden * hidden * hidden)
    tangent = jnp.tanh(inner)
    value = 0.5 * hidden * (1.0 + tangent)
    slope = 0.5 * (1.0 + tangent) + 0.5 * hidden * (1.0 - tangent * tangent) * 0.7978845608 * (
        1.0 + 3.0 * 0.044715 * hidden * hidden
    )
    return (value, slope)


def contract(left, right, left_dim, right_dim):
    return lax.dot_general(
        left, right, (((left_dim,), (right_dim,)), ((), ())), preferred_element_type=jnp.float32
    )


def hidden_side(left, weight, weight_dim):
    return lax.psum_scatter(
        contract(left, weight, 1, weight_dim), "col", scatter_dimension=0, tiled=True
    )


def spread_rows(local):
    return lax.all_gather(local, "col", axis=0, tiled=True)


def width_side(left, weight, weight_dim):
    return lax.psum_scatter(
        contract(left, weight, 1, weight_dim), ("row", "depth"), scatter_dimension=0, tiled=True
    )


def shards(inputs, w_in, w_out, grad_out):
    rows_in, rows_grad = (
        lax.all_gather(inputs, ("row", "depth"), axis=0, tiled=True),
        lax.all_gather(grad_out, ("row", "depth"), axis=0, tiled=True),
    )
    factor = 1.0 / rows_in.shape[0] ** 0.5
    hidden = hidden_side(rows_in, w_in, 0)
    value, slope = gelu_parts(hidden)
    act = value.astype(jnp.bfloat16)
    act_rows = spread_rows(act)
    outputs = width_side(act_rows, w_out, 0).astype(jnp.bfloat16)
    grad_act = hidden_side(rows_grad, w_out, 1)
    grad_hidden = (grad_act * slope).astype(jnp.bfloat16)
    grad_rows = spread_rows(grad_hidden)
    grad_in = width_side(grad_rows, w_in, 1).astype(jnp.bfloat16)
    grad_w_in = (contract(rows_in, grad_rows, 0, 0) * factor).astype(jnp.bfloat16)
    grad_w_out = (contract(act_rows, rows_grad, 0, 0) * factor).astype(jnp.bfloat16)
    return (outputs, grad_in, grad_w_in, grad_w_out)


def solution(mesh):
    in_specs = (
        P(("row", "depth"), "col"),
        P("col", ("row", "depth")),
        P(("row", "depth"), "col"),
        P(("row", "depth"), "col"),
    )
    out_specs = (
        P(("row", "depth"), "col"),
        P(("row", "depth"), "col"),
        P("col", ("row", "depth")),
        P(("row", "depth"), "col"),
    )
    return jax.shard_map(shards, mesh=mesh, in_specs=in_specs, out_specs=out_specs, check_vma=False)
```

profile of v0, /device:TPU:1, one launch (start us, length us, event | category | flops | bytes accessed | tf_op | source)
XLA Modules:
  0.0 413.7 jit_solution(7079718064812970021)
XLA Ops:
  7.2 0.0 copy-start
  7.2 0.0 all-gather.5.cloned.1.call-start
  7.2 0.7 all-gather.5.cloned.1.call-update
  7.9 0.0 all-gather.3.cloned.1.call-start
  8.0 0.7 all-gather.3.cloned.1.call-update
  8.7 0.0 reduce-scatter.9.cloned.1.call-start
  8.7 54.4 %all-gather.5.cloned.1.call-done = bf16[512,1536]{1,0:T(8,128)(2,1)} async-done(((bf16[16,1536]{1,0:T(8,128)(2,1)}), bf16[512,1536]{1,0:T(8,128)(2,1)}) %all-gather.5.cloned.1.call-update) | async-done | bytes 1572880 | tf_op jit(solution)/shard_map/all_gather | solution.py:42
  63.1 4.0 fusion.10
  67.0 0.0 reduce-scatter.9.cloned.1.call-update
  67.1 0.0 reduce-scatter.5.cloned.1.call-start
  67.1 46.2 %all-gather.3.cloned.1.call-done = bf16[512,1536]{1,0:T(8,128)(2,1)} async-done(((bf16[16,1536]{1,0:T(8,128)(2,1)}), bf16[512,1536]{1,0:T(8,128)(2,1)}) %all-gather.3.cloned.1.call-update) | async-done | bytes 1572880 | tf_op jit(solution)/shard_map/all_gather | solution.py:41
  113.3 4.7 %fusion.8 = f32[512,768]{1,0:T(8,128)} fusion(bf16[512,1536]{1,0:T(8,128)(2,1)} %all-gather.3.cloned.1.call-done, bf16[1536,768]{1,0:T(8,128)(2,1)} %param.5), kind=kOutput, calls=%fused_computation.13 | convolution fusion | flops 1207959552 | bytes 5505024 | tf_op jit(solution)/shard_map/dot_general | solution.py:18
  118.0 0.0 reduce-scatter.5.cloned.1.call-update
  118.0 0.0 reduce-scatter.7.cloned.1.call-start
  118.0 33.7 %reduce-scatter.9.cloned.1.call-done = f32[64,768]{1,0:T(8,128)} async-done(((f32[512,768]{1,0:T(8,128)}), f32[64,768]{1,0:T(8,128)}) %reduce-scatter.9.cloned.1.call-update) | async-done | bytes 196624 | tf_op jit(solution)/shard_map/reduce_scatter | solution.py:24
  151.7 42.1 %reduce-scatter.5.cloned.1.call-done = f32[64,768]{1,0:T(8,128)} async-done(((f32[512,768]{1,0:T(8,128)}), f32[64,768]{1,0:T(8,128)}) %reduce-scatter.5.cloned.1.call-update) | async-done | bytes 196624 | tf_op jit(solution)/shard_map/reduce_scatter | solution.py:24
  193.9 1.2 fusion.7
  195.0 20.4 %all_gather.13 = bf16[512,768]{1,0:T(8,128)(2,1)S(1)} all-gather(bf16[64,768]{1,0:T(8,128)(2,1)S(1)} %get-tuple-element.9), channel_id=1, replica_groups=mesh['row'=4,'col'=8,'depth'=8] {'col'}, dimensions={0}, use_global_device_ids=true | all-gather | bytes 884736 | tf_op jit(solution)/shard_map/all_gather | solution.py:30
  215.5 3.0 fusion.9
  218.5 0.0 reduce-scatter.7.cloned.1.call-update
  218.5 0.0 reduce-scatter.11.cloned.1.call-start
  218.6 19.4 %all_gather.15 = bf16[512,768]{1,0:T(8,128)(2,1)S(1)} all-gather(bf16[64,768]{1,0:T(8,128)(2,1)S(1)} %get-tuple-element.8), channel_id=1, replica_groups=mesh['row'=4,'col'=8,'depth'=8] {'col'}, dimensions={0}, use_global_device_ids=true | all-gather | bytes 884736 | tf_op jit(solution)/shard_map/all_gather | solution.py:30
  237.9 0.9 copy-done.1
  238.8 4.8 %fusion.11 = f32[512,1536]{1,0:T(8,128)} fusion(bf16[512,768]{1,0:T(8,128)(2,1)S(1)} %all_gather.15, bf16[1536,768]{1,0:T(8,128)(2,1)} %param.5), kind=kOutput, calls=%fused_computation.16 | convolution fusion | flops 1207959552 | bytes 6291456 | tf_op jit(solution)/shard_map/dot_general | solution.py:18
  243.6 0.0 reduce-scatter.11.cloned.1.call-update
  243.7 4.5 %fusion = bf16[1536,768]{0,1:T(8,128)(2,1)} fusion(bf16[512,768]{1,0:T(8,128)(2,1)} %copy-done.1, bf16[512,1536]{1,0:T(8,128)(2,1)} %all-gather.3.cloned.1.call-done), kind=kOutput, calls=%fused_computation.2 | convolution fusion | flops 1210318848 | bytes 4718592 | tf_op jit(solution)/shard_map/dot_general | solution.py:18
  248.2 4.3 %copy.8 = bf16[1536,768]{1,0:T(8,128)(2,1)} copy(bf16[1536,768]{0,1:T(8,128)(2,1)} %fusion) | data formatting | bytes 4718592
  252.5 4.3 %multiply_convert_fusion = bf16[768,1536]{1,0:T(8,128)(2,1)} fusion(bf16[512,768]{1,0:T(8,128)(2,1)S(1)} %all_gather.13, bf16[512,1536]{1,0:T(8,128)(2,1)} %all-gather.5.cloned.1.call-done), kind=kOutput, calls=%fused_computation | convolution fusion | flops 1210318848 | bytes 4718592 | tf_op jit(solution)/shard_map/dot_general | solution.py:18
  256.7 56.9 %reduce-scatter.7.cloned.1.call-done = f32[16,1536]{1,0:T(8,128)} async-done(((f32[512,1536]{1,0:T(8,128)}), f32[16,1536]{1,0:T(8,128)}) %reduce-scatter.7.cloned.1.call-update) | async-done | bytes 98320 | tf_op jit(solution)/shard_map/reduce_scatter | solution.py:34
  313.6 1.5 convert_element_type.22
  315.1 90.2 %reduce-scatter.11.cloned.1.call-done = f32[16,1536]{1,0:T(8,128)} async-done(((f32[512,1536]{1,0:T(8,128)}), f32[16,1536]{1,0:T(8,128)}) %reduce-scatter.11.cloned.1.call-update) | async-done | bytes 98320 | tf_op jit(solution)/shard_map/reduce_scatter | solution.py:34
  405.3 1.5 convert_element_type.24
  (2 shorter events, 0.0 us)
Async XLA Ops:
  7.2 55.9 %copy-start = (bf16[768,1536]{1,0:T(8,128)(2,1)S(1)}, bf16[768,1536]{1,0:T(8,128)(2,1)}, u32[]{:S(2)}) copy-start(bf16[768,1536]{1,0:T(8,128)(2,1)} %param.6) | copy-start | bytes 7077892
  7.2 55.9 %all-gather.5.cloned.1.call-start = ((), (), s32[]{:S(2)}) async-start(), calls=%async_computation.7 | async-start | bytes 1622016 | tf_op jit(solution)/shard_map/all_gather | solution.py:42
  7.9 105.4 %all-gather.3.cloned.1.call-start = ((), (), s32[]{:S(2)}) async-start(), calls=%async_computation.4 | async-start | bytes 1622016 | tf_op jit(solution)/shard_map/all_gather | solution.py:41
  8.7 143.1 %reduce-scatter.9.cloned.1.call-start = ((), (), s32[]{:S(2)}) async-start(), calls=%async_computation.8 | async-start | bytes 1769472 | tf_op jit(solution)/shard_map/reduce_scatter | solution.py:24
  67.1 126.8 %reduce-scatter.5.cloned.1.call-start = ((), (), s32[]{:S(2)}) async-start(), calls=%async_computation.5 | async-start | bytes 1769472 | tf_op jit(solution)/shard_map/reduce_scatter | solution.py:24
  118.0 195.6 %reduce-scatter.7.cloned.1.call-start = ((), (), s32[]{:S(2)}) async-start(), calls=%async_computation.6 | async-start | bytes 3244032 | tf_op jit(solution)/shard_map/reduce_scatter | solution.py:34
  218.5 186.8 %reduce-scatter.11.cloned.1.call-start = ((), (), s32[]{:S(2)}) async-start(), calls=%async_computation.9 | async-start | bytes 3244032 | tf_op jit(solution)/shard_map/reduce_scatter | solution.py:34
  237.9 0.9 copy-start.1
Sparse Core Ops, SparseCore 0:
  10.6 52.4 all-gather.4
  65.6 47.6 all-gather.2
  116.4 35.2 reduce-scatter.8
  154.7 39.1 reduce-scatter.4
  218.6 94.9 reduce-scatter.6
  317.9 87.3 reduce-scatter.10
where the time goes:
time: 415 us; the launch traced here: 414 us
  waiting for transfers between devices  325 us (78%)
  blocking collectives  39.8 us (10%)
  matrix products  25.3 us (6%)
  between operations  14.1 us (3%)
  local copies, waits for them, and re-layouts  5.19 us (1%)
  other arithmetic  4.19 us (1%)
    reduce_scatter x2, waiting for transfers between devices, width_side(): lax.psum_scatter(contract(left, weight, 1, weight_dim), ('row', 'depth'),...  147 us
    reduce_scatter x2, waiting for transfers between devices, hidden_side(): lax.psum_scatter(contract(left, weight, 1, weight_dim), 'col', scatter_di...  75.8 us
    all_gather x1, waiting for transfers between devices, shards(): lax.all_gather(grad_out, ('row', 'depth'), axis=0, tiled=True)  54.4 us
    all_gather x1, waiting for transfers between devices, shards(): lax.all_gather(inputs, ('row', 'depth'), axis=0, tiled=True)  46.2 us
    all_gather x2, blocking collectives, spread_rows(): return lax.all_gather(local, 'col', axis=0, tiled=True)  39.8 us
    dot_general x6, matrix products, contract(): lax.dot_general(left, right, (((left_dim,), (right_dim,)), ((), ())), pre...  25.3 us
  transfers between devices with their start and end apart: 6, of which 6 were waited for; matrix products, arithmetic and copies ran while one was open for 7% of the time, Pallas kernels for 0%

commit v1 on v0

v1 whole, which is shorter than its diff:
```python
import functools

import jax
import jax.numpy as jnp
from jax import lax
from jax.experimental import pallas as pl
from jax.experimental.pallas import tpu as pltpu
from jax.sharding import PartitionSpec as P

MESH = pl.DeviceIdType.MESH
BF = jnp.bfloat16
F32 = jnp.float32


def gelu_parts(hidden):
    inner = 0.7978845608 * (hidden + 0.044715 * hidden * hidden * hidden)
    tangent = jnp.tanh(inner)
    value = 0.5 * hidden * (1.0 + tangent)
    slope = 0.5 * (1.0 + tangent) + 0.5 * hidden * (1.0 - tangent * tangent) * 0.7978845608 * (
        1.0 + 3.0 * 0.044715 * hidden * hidden
    )
    return (value, slope)


def contract(left, right, left_dim, right_dim):
    return lax.dot_general(
        left, right, (((left_dim,), (right_dim,)), ((), ())), preferred_element_type=F32
    )


def body(
    n, nz, factor,
    x_hbm, win_hbm, wout_hbm, g_hbm,
    out_ref, gin_ref, gwin_hbm, gwout_hbm,
    acts, win, wout, part, z_send, z_recv, slope_ref, wide,
    own_sum, oth_sum, sib_sum, p1_send, p1_recv, p2_send, p2_recv, fin_send, fin_recv,
    gw_in, gw_out,
    w_sem, gw_sem,
    s1_ssem, s1_rsem, s2_ssem, s2_rsem, sp_ssem, sp_rsem,
    z_ssem, z_rsem, a_ssem, a_rsem,
    sib_ssem, sib_rsem, p1_ssem, p1_rsem, p2_ssem, p2_rsem, fin_ssem, fin_rsem,
):
    y = lax.axis_index("row")
    z = lax.axis_index("col")
    depth = lax.axis_index("depth")
    x, c = depth // 2, lax.rem(depth, 2)
    o = 1 - c
    half = win.shape[1]
    mid = half // 2
    width = win.shape[2]
    wmid = width // 2

    def at(xx, yy, zz, cc):
        return (lax.rem(yy, n), lax.rem(zz, nz), lax.rem(xx, n) * 2 + cc)

    sibling = at(x, y, z, o)
    right, left = at(x, y, z + 1, c), at(x, y, z + nz - 1, c)

    def line1(d):
        return at(x + d * o, y + d * c, z, c)

    def line2(d):
        return at(x + d * c, y + d * o, z, c)

    q1, q2 = x * o + y * c, y * o + x * c
    r1, r2 = q2, q1

    def back(q, d):
        return lax.rem(q + (n - d), n)

    def ahead(q, d):
        return lax.rem(q + d, n)

    def remote(src, dst, ssem, rsem, device):
        return pltpu.make_async_remote_copy(
            src_ref=src, dst_ref=dst, send_sem=ssem, recv_sem=rsem, device_id=device, device_id_type=MESH
        )

    w_copies = []
    for h in range(2):
        w_copies.append(pltpu.make_async_copy(win_hbm.at[pl.ds(h * half, half), :], win.at[h], w_sem.at[0, h]))
        w_copies.append(pltpu.make_async_copy(wout_hbm.at[:, pl.ds(h * half, half)], wout.at[h], w_sem.at[1, h]))
    w_copies = [w_copies[0], w_copies[2], w_copies[1], w_copies[3]]
    for copy in w_copies:
        copy.start()

    barrier = pltpu.get_barrier_semaphore()
    partners = [sibling, right, left]
    for d in range(1, n):
        for cc in range(2):
            partners.append(at(x + d, y, z, cc))
            partners.append(at(x, y + d, z, cc))
    for partner in partners:
        pl.semaphore_signal(barrier, inc=1, device_id=partner, device_id_type=MESH)
    pl.semaphore_wait(barrier, len(partners))

    pending = []

    def launch(copy):
        copy.start()
        pending.append(copy)
        return copy

    def drain(keep=0):
        while len(pending) > keep:
            pending.pop(0).wait_send()

    sources = (x_hbm, g_hbm)

    def s1(a):
        src = sources[a]
        for d in (2, 1, 3):
            if d >= n:
                continue
            launch(remote(src.at[:, pl.ds(0, half)], acts.at[a, 0, c, y, x], s1_ssem.at[a, 0, d], s1_rsem.at[a, c, d], at(x + d, y, z, 0)))
            launch(remote(src.at[:, pl.ds(half, half)], acts.at[a, 1, c, x, y], s1_ssem.at[a, 1, d], s1_rsem.at[a, c, d], at(x, y + d, z, 1)))
        theirs = src.at[:, pl.ds(pl.multiple_of(o * half, half), half)]
        mine = src.at[:, pl.ds(pl.multiple_of(c * half, half), half)]
        launch(remote(theirs, acts.at[a, o, c, r2, r1], s1_ssem.at[a, 0, 0], s1_rsem.at[a, c, 0], sibling))
        pltpu.make_async_copy(mine, acts.at[a, c, c, q2, q1], s1_rsem.at[a, c, 0]).start()

    def s2(a, t):
        for d in range(n):
            slot = acts.at[a, c, t, q2, back(q1, d)]
            pltpu.make_async_copy(slot, slot, s1_rsem.at[a, t, d]).wait()
        line = acts.at[a, c, t, q2]
        for d in (2, 1, 3):
            if d < n:
                launch(remote(line, line, s2_ssem.at[a, t, d], s2_rsem.at[a, t, d], line2(d)))
        launch(remote(line, line, sp_ssem.at[a, t, 0], sp_rsem.at[a, t, 0], sibling))

    def s3(a, t):
        for d in (1, 3, 2):
            if d >= n:
                continue
            line = acts.at[a, c, t, back(q2, d)]
            pltpu.make_async_copy(line, line, s2_rsem.at[a, t, d]).wait()
            launch(remote(line, line, sp_ssem.at[a, t, d], sp_rsem.at[a, t, d], sibling))
        for d in range(n):
            line = acts.at[a, o, t, back(r2, d)]
            pltpu.make_async_copy(line, line, sp_rsem.at[a, t, d]).wait()

    def rows_of(a, h, t):
        if h == 0:
            return acts[a, 0, t].reshape(n * n * 16, half)
        return jnp.concatenate([acts[a, 1, t, i, j] for j in range(n) for i in range(n)], axis=0)

    def partial(a, t):
        s = 2 * a + t
        rows = [rows_of(a, h, t) for h in range(2)]
        step = 256 if width % 256 == 0 else width
        for k in range(0, width, step):
            if a == 0:
                value = sum(contract(rows[h], win[h, :, k:k + step], 1, 0) for h in range(2))
            else:
                value = sum(contract(rows[h], wout[h, k:k + step, :], 1, 1) for h in range(2))
            part[s, :, :, k:k + step] = value.reshape(nz, -1, step)

    hz = nz // 2

    def rs_send(s, way, i, cols):
        ref = (s, way, i) if cols is None else (s, way, i, slice(None), cols)
        return remote(z_send.at[ref], z_recv.at[ref], z_ssem.at[s, way, i], z_rsem.at[s, way, i], (right, left)[way])

    rs = {}
    first_cols = (pl.ds(0, wmid), pl.ds(wmid, wmid))

    def rs_step(s, i):
        if i == 0:
            k = lax.rem(z + hz, nz)
            for way in range(2):
                cols = slice(way * wmid, (way + 1) * wmid)
                z_send[s, way, 0, :, cols] = part[s, k, :, cols].astype(BF)
                rs[s, way, 0] = launch(rs_send(s, way, 0, first_cols[way]))
            return
        if i < hz:
            for way in range(2):
                k = lax.rem(z + (hz - i if way == 0 else hz + i), nz)
                rs[s, way, i - 1].wait_recv()
                if i == 1:
                    for side in range(2):
                        cols = slice(side * wmid, (side + 1) * wmid)
                        value = part[s, k, :, cols]
                        if side == way:
                            value = value + z_recv[s, way, 0, :, cols].astype(F32)
                        z_send[s, way, i, :, cols] = value.astype(BF)
                else:
                    z_send[s, way, i] = (part[s, k] + z_recv[s, way, i - 1].astype(F32)).astype(BF)
                rs[s, way, i] = launch(rs_send(s, way, i, None))
            return
        rs[s, 0, hz - 1].wait_recv()
        rs[s, 1, hz - 1].wait_recv()
        total = part[s, z] + (z_recv[s, 0, hz - 1].astype(F32) + z_recv[s, 1, hz - 1].astype(F32))
        t = s % 2
        if s < 2:
            value, slope = gelu_parts(total)
            slope_ref[t] = slope
            wide[0, t, z] = value.astype(BF)
        else:
            wide[1, t, z] = (total * slope_ref[t]).astype(BF)

    ag = {}

    def ag_step(s, i):
        a, t = s // 2, s % 2
        if i > 0:
            ag[s, 0, i - 1].wait_recv()
            ag[s, 1, i - 1].wait_recv()
        if i == hz:
            return
        for way in range(2):
            k = lax.rem(z + (nz - i if way == 0 else i), nz)
            block = wide.at[a, t, k]
            if i == hz - 1:
                block = wide.at[a, t, k, pl.ds(16 * way, 16)]
            ag[s, way, i] = launch(remote(block, block, a_ssem.at[s, way, i], a_rsem.at[s, way, i], (right, left)[way]))

    sib = {}

    def product(s):
        a, t = s // 2, s % 2
        rows = wide[a, t].reshape(-1, width)
        for which, ref in ((o, oth_sum), (c, own_sum)):
            step = 256 if half % 256 == 0 else half
            for k in range(0, half, step):
                if a == 0:
                    value = contract(rows, wout[which, :, k:k + step], 1, 0)
                else:
                    value = contract(rows, win[which, k:k + step, :], 1, 1)
                ref[s, :, :, k:k + step] = value.reshape(n * n, 16, step)
            if ref is oth_sum:
                sib[s] = launch(remote(oth_sum.at[s], sib_sum.at[s], sib_ssem.at[s], sib_rsem.at[s], sibling))

    def block_of(i1, i2):
        return i1 * (1 + (n - 1) * c) + i2 * (n - (n - 1) * c)

    p1, p2 = {}, {}

    def phase1(s):
        sib[s].wait_recv()
        for d in (2, 1, 3):
            if d >= n:
                continue
            i1 = ahead(q1, d)
            for j in range(n):
                b = block_of(i1, j)
                p1_send[s, d - 1, j] = (own_sum[s, b] + sib_sum[s, b]).astype(BF)
            p1[s, d] = launch(remote(p1_send.at[s, d - 1], p1_recv.at[s, d - 1], p1_ssem.at[s, d], p1_rsem.at[s, d], line1(d)))

    def line_total(s, j):
        b = block_of(q1, j)
        value = own_sum[s, b] + sib_sum[s, b]
        for d in range(1, n):
            value = value + p1_recv[s, d - 1, j].astype(F32)
        return value

    def phase2(s):
        for d in range(1, n):
            p1[s, d].wait_recv()
        for d in (2, 1, 3):
            if d >= n:
                continue
            p2_send[s, d - 1] = line_total(s, ahead(q2, d))
            p2[s, d] = launch(remote(p2_send.at[s, d - 1], p2_recv.at[s, d - 1], p2_ssem.at[s, d], p2_rsem.at[s, d], line2(d)))

    results = (out_ref, gin_ref)

    def finish(s):
        a, t = s // 2, s % 2
        value = line_total(s, q2)
        for d in range(1, n):
            p2[s, d].wait_recv()
        for d in range(1, n):
            value = value + p2_recv[s, d - 1]
        value = value.astype(BF)

        @pl.when(c != t)
        def _():
            fin_send[a] = value
            remote(fin_send.at[a], fin_recv.at[a], fin_ssem.at[a], fin_rsem.at[a], sibling).start()

        @pl.when(c == t)
        def _():
            cols = slice(t * half, (t + 1) * half)
            results[a][:, cols] = value

    def collect(a):
        copy = remote(fin_send.at[a], fin_recv.at[a], fin_ssem.at[a], fin_rsem.at[a], sibling)
        copy.wait_send()
        copy.wait_recv()
        for t in range(2):
            @pl.when(c == t)
            def _():
                cols = slice((1 - t) * half, (2 - t) * half)
                results[a][:, cols] = fin_recv[a]

    gw_copies = []

    def grad_w_out(h):
        cols = jnp.concatenate([rows_of(1, h, t) for t in range(2)], axis=0)
        step = 256 if width % 256 == 0 else width
        for k in range(0, width, step):
            left_rows = wide[0, :, :, :, k:k + step].reshape(-1, step)
            gw_out[h, k:k + step, :] = (contract(left_rows, cols, 0, 0) * factor).astype(BF)
        copy = pltpu.make_async_copy(gw_out.at[h], gwout_hbm.at[:, pl.ds(h * half, half)], gw_sem.at[1, h])
        copy.start()
        gw_copies.append(copy)

    def grad_w_in(h):
        cols = wide[1].reshape(-1, width)
        step = 256 if half % 256 == 0 else half
        rows = jnp.concatenate([rows_of(0, h, t) for t in range(2)], axis=0)
        for k in range(0, half, step):
            gw_in[h, k:k + step, :] = (contract(rows[:, k:k + step], cols, 0, 0) * factor).astype(BF)
        copy = pltpu.make_async_copy(gw_in.at[h], gwin_hbm.at[pl.ds(h * half, half), :], gw_sem.at[0, h])
        copy.start()
        gw_copies.append(copy)

    s1(0)
    s2(0, 0)
    s2(0, 1)
    s1(1)
    s3(0, 0)
    w_copies[0].wait()
    w_copies[1].wait()
    partial(0, 0)
    rs_step(0, 0)
    s2(1, 0)
    s3(0, 1)
    partial(0, 1)
    rs_step(1, 0)
    s2(1, 1)
    rs_step(0, 1)
    s3(1, 0)
    w_copies[2].wait()
    w_copies[3].wait()
    partial(1, 0)
    rs_step(2, 0)
    rs_step(1, 1)
    rs_step(0, 2)
    s3(1, 1)
    partial(1, 1)
    rs_step(3, 0)
    rs_step(1, 2)
    rs_step(2, 1)
    rs_step(0, 3)
    rs_step(3, 1)
    rs_step(1, 3)
    rs_step(2, 2)
    rs_step(0, 4)
    ag_step(0, 0)
    rs_step(3, 2)
    rs_step(1, 4)
    ag_step(1, 0)
    rs_step(2, 3)
    ag_step(0, 1)
    rs_step(3, 3)
    ag_step(1, 1)
    rs_step(2, 4)
    ag_step(2, 0)
    ag_step(0, 2)
    rs_step(3, 4)
    ag_step(3, 0)
    ag_step(1, 2)
    ag_step(2, 1)
    ag_step(0, 3)
    ag_step(3, 1)
    ag_step(1, 3)
    ag_step(2, 2)
    ag_step(0, 4)
    product(0)
    ag_step(3, 2)
    ag_step(1, 4)
    product(1)
    ag_step(2, 3)
    phase1(0)
    ag_step(3, 3)
    phase1(1)
    ag_step(2, 4)
    product(2)
    phase2(0)
    ag_step(3, 4)
    product(3)
    phase1(2)
    phase2(1)
    phase1(3)
    grad_w_out(0)
    finish(0)
    phase2(2)
    grad_w_out(1)
    finish(1)
    phase2(3)
    grad_w_in(0)
    finish(2)
    grad_w_in(1)
    finish(3)
    drain()
    collect(0)
    collect(1)
    for copy in gw_copies:
        copy.wait()


def shards(n, nz, inputs, w_in, w_out, grad_out):
    rows, wide_cols = inputs.shape
    half = wide_cols // 2
    width = w_in.shape[1]
    tokens = 2 * n * n * rows
    chunk = n * n * rows // nz
    any_spec = pl.BlockSpec(memory_space=pl.ANY)
    vmem_spec = pl.BlockSpec(memory_space=pltpu.VMEM)
    dma = pltpu.SemaphoreType.DMA
    hz = nz // 2
    scratch = [
        pltpu.VMEM((2, 2, 2, n, n, rows, half), BF),
        pltpu.VMEM((2, half, width), BF),
        pltpu.VMEM((2, width, half), BF),
        pltpu.VMEM((4, nz, chunk, width), F32),
        pltpu.VMEM((4, 2, hz, chunk, width), BF),
        pltpu.VMEM((4, 2, hz, chunk, width), BF),
        pltpu.VMEM((2, chunk, width), F32),
        pltpu.VMEM((2, 2, nz, chunk, width), BF),
        pltpu.VMEM((4, n * n, rows, half), F32),
        pltpu.VMEM((4, n * n, rows, half), F32),
        pltpu.VMEM((4, n * n, rows, half), F32),
        pltpu.VMEM((4, n - 1, n, rows, half), BF),
        pltpu.VMEM((4, n - 1, n, rows, half), BF),
        pltpu.VMEM((4, n - 1, rows, half), F32),
        pltpu.VMEM((4, n - 1, rows, half), F32),
        pltpu.VMEM((2, rows, half), BF),
        pltpu.VMEM((2, rows, half), BF),
        pltpu.VMEM((2, half, width), BF),
        pltpu.VMEM((2, width, half), BF),
        dma((2, 2)), dma((2, 2)),
        dma((2, 2, n)), dma((2, 2, n)),
        dma((2, 2, n)), dma((2, 2, n)),
        dma((2, 2, n)), dma((2, 2, n)),
        dma((4, 2, hz)), dma((4, 2, hz)),
        dma((4, 2, hz)), dma((4, 2, hz)),
        dma((4,)), dma((4,)),
        dma((4, n)), dma((4, n)),
        dma((4, n)), dma((4, n)),
        dma((2,)), dma((2,)),
    ]
    return pl.pallas_call(
        functools.partial(body, n, nz, 1.0 / tokens ** 0.5),
        name="ffn",
        out_shape=(
            jax.ShapeDtypeStruct(inputs.shape, BF),
            jax.ShapeDtypeStruct(inputs.shape, BF),
            jax.ShapeDtypeStruct(w_in.shape, BF),
            jax.ShapeDtypeStruct(w_out.shape, BF),
        ),
        in_specs=[any_spec] * 4,
        out_specs=(vmem_spec, vmem_spec, any_spec, any_spec),
        scratch_shapes=scratch,
        compiler_params=pltpu.CompilerParams(
            collective_id=0, has_side_effects=True, vmem_limit_bytes=60 * 2 ** 20
        ),
        cost_estimate=pl.CostEstimate(
            flops=12 * tokens * wide_cols * width, bytes_accessed=8 * wide_cols * width, transcendentals=0
        ),
    )(inputs, w_in, w_out, grad_out)


def solution(mesh):
    n, nz = mesh.shape["row"], mesh.shape["col"]
    in_specs = (
        P(("row", "depth"), "col"),
        P("col", ("row", "depth")),
        P(("row", "depth"), "col"),
        P(("row", "depth"), "col"),
    )
    out_specs = (
        P(("row", "depth"), "col"),
        P(("row", "depth"), "col"),
        P("col", ("row", "depth")),
        P(("row", "depth"), "col"),
    )
    return jax.shard_map(
        functools.partial(shards, n, nz), mesh=mesh, in_specs=in_specs, out_specs=out_specs, check_vma=False
    )
```

time: 415 us -> 90.1 us (0.22)
  waiting for transfers between devices: 325 us -> 0 us
  Pallas kernels: 0 us -> 81.6 us
  blocking collectives: 39.8 us -> 0 us
  matrix products: 25.3 us -> 0 us
  between operations: 14.1 us -> 0.64 us
  other arithmetic: 4.19 us -> 0 us
    reduce_scatter x4 -> x0, waiting for transfers between devices: 223 us -> none  [the longest x2 147 us: width_side(): lax.psum_scatter(contract(left, weight, 1, weight_dim), ('row', 'depth'),...]
    all_gather x2 -> x0, waiting for transfers between devices: 101 us -> none  [the longest x1 54.4 us: shards(): lax.all_gather(grad_out, ('row', 'depth'), axis=0, tiled=True)]
    pallas_call x0 -> x1, Pallas kernels: none -> 81.6 us  [shards(): pl.pallas_call(functools.partial(body, n, nz, 1.0 / tokens ** 0.5), name=...]
    all_gather x2 -> x0, blocking collectives: 39.8 us -> none  [spread_rows(): return lax.all_gather(local, 'col', axis=0, tiled=True)]
    dot_general x6 -> x0, matrix products: 25.3 us -> none  [contract(): lax.dot_general(left, right, (((left_dim,), (right_dim,)), ((), ())), pre...]
    convert_element_type x3 -> x0, other arithmetic: 4.19 us -> none  [the longest x1 1.52 us: shards(): outputs = width_side(act_rows, w_out, 0).astype(jnp.bfloat16)]
  transfers between devices with their start and end apart: 6 -> 0, of which waited for: 6 -> 0; matrix products, arithmetic and copies ran while one was open for 7% -> 0% of each run, Pallas kernels for 0% -> 0%
where the time goes in v1:
time: 90.1 us; the launch traced here: 89.8 us
  Pallas kernels  81.6 us (91%)
  local copies, waits for them, and re-layouts  7.62 us (8%)
    pallas_call x1, Pallas kernels, shards(): pl.pallas_call(functools.partial(body, n, nz, 1.0 / tokens ** 0.5), name=...  81.6 us
    unnamed x6, local copies, waits for them, and re-layouts  7.62 us

profile of v1, /device:TPU:1, one launch (start us, length us, event | category | flops | bytes accessed | tf_op | source)
XLA Modules:
  0.0 89.8 jit_solution(1258767705589534603)
XLA Ops:
  0.6 81.6 %ffn.1 = (bf16[16,1536]{1,0:T(8,128)(2,1)}, bf16[16,1536]{1,0:T(8,128)(2,1)}, bf16[1536,768]{1,0:T(8,128)(2,1)}, bf16[768,1536]{1,0:T(8,128)(2,1)}) custom-call(bf16[16,1536]{1,0:T(8,128)(2,1)} %x_hbm.1, bf16[1536,768]{1,0:T(8,128)(2,1)} %win_hbm.1, bf16[768,1536]{1,0:T(8,128)(2,1)} %wout_hbm.1, bf16[16,1536]{1,0:T(8,128)(2,1)} %g_hbm.1), custom_call_target="tpu_custom_call" | custom-call | flops 7247757312 | bytes 9437184 | tf_op jit(solution)/shard_map/ffn/pallas_call | solution.py:445
  82.2 1.4 %copy.12 = bf16[16,1536]{1,0:T(8,128)(2,1)} copy(bf16[16,1536]{1,0:T(8,128)(2,1)} %get-tuple-element.8) | data formatting | bytes 98304
  83.6 1.4 %copy.13 = bf16[16,1536]{1,0:T(8,128)(2,1)} copy(bf16[16,1536]{1,0:T(8,128)(2,1)} %get-tuple-element.9) | data formatting | bytes 98304
  85.1 0.0 copy-start
  85.1 3.4 %copy.14 = bf16[1536,768]{1,0:T(8,128)(2,1)} copy(bf16[1536,768]{1,0:T(8,128)(2,1)} %get-tuple-element.10) | data formatting | bytes 4718592
  88.4 0.0 copy-done
  88.4 1.4 %copy.15 = bf16[768,1536]{1,0:T(8,128)(2,1)} copy(bf16[768,1536]{1,0:T(8,128)(2,1)S(1)} %copy-done) | data formatting | bytes 4718592
Async XLA Ops:
  85.1 3.4 %copy-start = (bf16[768,1536]{1,0:T(8,128)(2,1)S(1)}, bf16[768,1536]{1,0:T(8,128)(2,1)}, u32[]{:S(2)}) copy-start(bf16[768,1536]{1,0:T(8,128)(2,1)} %get-tuple-element.11) | copy-start | bytes 7077892

commit v2 on v0

v2 whole, which is shorter than its diff:
```python
import functools

import jax
import jax.numpy as jnp
from jax import lax
from jax.experimental import pallas as pl
from jax.experimental.pallas import tpu as pltpu
from jax.sharding import PartitionSpec as P

MESH = pl.DeviceIdType.MESH
BF = jnp.bfloat16
F32 = jnp.float32


SHORT_SUMS = (0,)
SHORT_GATHERS = ()

SCHEDULE = (
    ("s1", 0), ("s1", 1), ("s2", 0, 1), ("s2", 0, 0), ("s2", 1, 0), ("s2", 1, 1), ("s3", 0, 1), ("s4", 0, 1),
    ("weights", 0), ("partial", 0, 1), ("s3", 0, 0), ("rs_step", 1, 0), ("s4", 0, 0), ("partial", 0, 0),
    ("rs_step", 0, 0), ("s3", 1, 0), ("rs_step", 1, 1), ("s3", 1, 1), ("s4", 1, 0), ("weights", 1), ("partial", 1, 0),
    ("rs_step", 2, 0), ("s4", 1, 1), ("partial", 1, 1), ("rs_step", 3, 0), ("rs_step", 0, 1), ("rs_step", 1, 2),
    ("rs_step", 2, 1), ("rs_step", 3, 1), ("rs_step", 0, 2), ("ag_step", 0, 0), ("rs_step", 1, 3), ("rs_step", 2, 2),
    ("rs_step", 3, 2), ("ag_step", 0, 1), ("rs_step", 1, 4), ("ag_step", 1, 0), ("rs_step", 2, 3), ("rs_step", 3, 3),
    ("ag_step", 0, 2), ("ag_step", 1, 1), ("rs_step", 2, 4), ("ag_step", 2, 0), ("rs_step", 3, 4), ("ag_step", 3, 0),
    ("ag_step", 0, 3), ("product", 0, True), ("ag_step", 1, 2), ("ag_step", 2, 1), ("ag_step", 3, 1),
    ("ag_step", 0, 4), ("product", 0, False), ("ag_step", 1, 3), ("product", 1, True), ("spread", 0),
    ("ag_step", 3, 2), ("ag_step", 2, 2), ("ag_step", 1, 4), ("grad_w_out", 1), ("product", 1, False),
    ("grad_w_out", 0), ("ag_step", 3, 3), ("product", 3, True), ("spread", 1), ("ag_step", 2, 3),
    ("product", 2, True), ("finish", 0), ("ag_step", 3, 4), ("product", 3, False), ("ag_step", 2, 4),
    ("product", 2, False), ("spread", 3), ("grad_w_in", 1), ("spread", 2), ("finish", 1), ("grad_w_in", 0),
    ("collect", 0), ("finish", 3), ("finish", 2), ("collect", 1), ("drain",),
)


def gelu_parts(hidden):
    inner = 0.7978845608 * (hidden + 0.044715 * hidden * hidden * hidden)
    tangent = jnp.tanh(inner)
    value = 0.5 * hidden * (1.0 + tangent)
    slope = 0.5 * (1.0 + tangent) + 0.5 * hidden * (1.0 - tangent * tangent) * 0.7978845608 * (
        1.0 + 3.0 * 0.044715 * hidden * hidden
    )
    return (value, slope)


def contract(left, right, left_dim, right_dim):
    return lax.dot_general(
        left, right, (((left_dim,), (right_dim,)), ((), ())), preferred_element_type=F32
    )


def body(
    n, nz, factor,
    x_hbm, win_hbm, wout_hbm, g_hbm,
    out_ref, gin_ref, gw_in, gw_out,
    acts, win, wout, part, z_send, z_recv, slope_ref, wide,
    own_sum, oth_sum, sib_sum, out_send, out_recv, fin_send, fin_recv,
    own_rows,
    w_sem, x_sem, s1_rsem, s2_rsem, sp_rsem, z_rsem, a_rsem, sib_rsem, out_rsem, fin_rsem, send_sem,
):
    y = lax.axis_index("row")
    z = lax.axis_index("col")
    depth = lax.axis_index("depth")
    x, c = depth // 2, lax.rem(depth, 2)
    o = 1 - c
    half = win.shape[1]
    quarter = half // 2
    width = win.shape[2]
    wmid = width // 2

    def at(xx, yy, zz, cc):
        return (lax.rem(yy, n), lax.rem(zz, nz), lax.rem(xx, n) * 2 + cc)

    sibling = at(x, y, z, o)
    hop = [[at(x, y, z + d, c) for d in (1, nz - 1)], [at(x, y, z + d, c) for d in (2, nz - 2)]]

    places = ((x, y), (y, x))

    def line(q, axis, d):
        return at(x + d, y, z, c) if q == axis else at(x, y + d, z, c)

    def back(q, d):
        return lax.rem(q + (n - d), n)

    def ahead(q, d):
        return lax.rem(q + d, n)

    def remote(src, dst, ssem, rsem, device):
        return pltpu.make_async_remote_copy(
            src_ref=src, dst_ref=dst, send_sem=ssem, recv_sem=rsem, device_id=device, device_id_type=MESH
        )

    x_copies, w_copies = [], []
    for a, src in enumerate((x_hbm, g_hbm)):
        for h in range(2):
            for q in range(2):
                cols = pl.ds(h * half + q * quarter, quarter)
                x_copies.append(pltpu.make_async_copy(src.at[:, cols], own_rows.at[a, h, q], x_sem.at[a]))
    for h in range(2):
        w_copies.append(pltpu.make_async_copy(win_hbm.at[pl.ds(h * half, half), :], win.at[h], w_sem.at[0]))
        w_copies.append(pltpu.make_async_copy(wout_hbm.at[:, pl.ds(h * half, half)], wout.at[h], w_sem.at[1]))
    for copy in x_copies + w_copies:
        copy.start()

    barrier = pltpu.get_barrier_semaphore()
    partners = [sibling]
    for d in sorted({1, 2, nz - 2, nz - 1}):
        partners.append(at(x, y, z + d, c))
    for d in range(1, n):
        for cc in range(2):
            partners.append(at(x + d, y, z, cc))
            partners.append(at(x, y + d, z, cc))
        for e in range(1, n):
            partners.append(at(x + d, y + e, z, c))
    for partner in partners:
        pl.semaphore_signal(barrier, inc=1, device_id=partner, device_id_type=MESH)
    pl.semaphore_wait(barrier, len(partners))

    def launch(copy):
        copy.start()
        return copy

    def arrived(ref, sem):
        pltpu.make_async_copy(ref, ref, sem).wait()

    def drain():
        blocks = own_sum
        for k, ref in enumerate((
            blocks.at[0, pl.ds(0, 2 * n - 1)],
            blocks.at[pl.ds(0, 2), pl.ds(0, n * (n - 1))],
            blocks.at[pl.ds(0, 2)],
            part.at[pl.ds(0, 2), pl.ds(0, nz - 1)],
            part.at[pl.ds(0, 2), pl.ds(0, nz - 1)],
            blocks.at[pl.ds(0, 2), pl.ds(0, n * n - 1)],
            fin_send,
            blocks.at[0], blocks.at[1], blocks.at[2], blocks.at[3],
        )):
            arrived(ref, send_sem.at[k])

    def s1(a):
        arrived(own_rows.at[a], x_sem.at[a])
        for d in (2, 1, 3):
            if d >= n:
                continue
            for h in range(2):
                for q in range(2):
                    first, second = places[q]
                    there = at(x + d, y, z, h) if q == 0 else at(x, y + d, z, h)
                    launch(remote(
                        own_rows.at[a, h, q], acts.at[a, h, q, c, second, first], send_sem.at[0], s1_rsem.at[a, c, q], there
                    ))
        for q in range(2):
            first, second = places[q]
            launch(remote(
                own_rows.at[a, o, q], acts.at[a, o, q, c, second, first], send_sem.at[0], s1_rsem.at[a, c, q], sibling
            ))
            launch(pltpu.make_async_copy(
                own_rows.at[a, c, q], acts.at[a, c, q, c, second, first], s1_rsem.at[a, c, q]
            ))

    def s2(a, t):
        for q in range(2):
            row = acts.at[a, c, q, t, places[q][1]]
            arrived(row, s1_rsem.at[a, t, q])
            for d in (2, 1, 3):
                if d < n:
                    launch(remote(row, row, send_sem.at[1], s2_rsem.at[a, t, q, d - 1], line(q, 1, d)))
            launch(remote(row, row, send_sem.at[2], sp_rsem.at[a, t], sibling))

    def s3(a, t):
        for d in (1, 3, 2):
            if d >= n:
                continue
            for q in range(2):
                row = acts.at[a, c, q, t, back(places[q][1], d)]
                arrived(row, s2_rsem.at[a, t, q, d - 1])
                launch(remote(row, row, send_sem.at[2], sp_rsem.at[a, t], sibling))

    def s4(a, t):
        arrived(acts.at[a, o, :, t], sp_rsem.at[a, t])

    def rows_of(a, h, t):
        across = [acts[a, h, 0, t].reshape(n * n * 16, quarter)]
        across.append(jnp.concatenate([acts[a, h, 1, t, i, j] for j in range(n) for i in range(n)], axis=0))
        return jnp.concatenate(across, axis=1)

    def partial(a, t):
        s = 2 * a + t
        rows = [rows_of(a, h, t) for h in range(2)]
        step = 256 if width % 256 == 0 else width
        for k in range(0, width, step):
            if a == 0:
                value = sum(contract(rows[h], win[h, :, k:k + step], 1, 0) for h in range(2))
            else:
                value = sum(contract(rows[h], wout[h, k:k + step, :], 1, 1) for h in range(2))
            part[s, :, :, k:k + step] = value.reshape(nz, -1, step)

    hz = nz // 2
    signs = (1, -1)

    def chunk_at(d):
        return lax.rem(z + (d + nz), nz)

    def rs_send(s, i, way, far):
        cols = (slice(None), pl.ds(0, wmid)) if i == 0 else ()
        ref = (s, way, i) + cols
        launch(remote(z_send.at[ref], z_recv.at[ref], send_sem.at[3], z_rsem.at[s, i], hop[far][way]))

    def rs_wait(s, i):
        ref = z_recv.at[s, :, 0, :, pl.ds(0, wmid)] if i == 0 else z_recv.at[s, :, i]
        arrived(ref, z_rsem.at[s, i])

    def rs_first(s, far):
        for way in range(2):
            z_send[s, way, 0, :, :wmid] = part[s, chunk_at(hz), :, way * wmid:(way + 1) * wmid].astype(BF)
            rs_send(s, 0, way, far)

    def with_half(s, way, value):
        half_in = z_recv[s, way, 0, :, :wmid].astype(F32)
        if way == 0:
            return jnp.concatenate([value[:, :wmid] + half_in, value[:, wmid:]], axis=1)
        return jnp.concatenate([value[:, :wmid], value[:, wmid:] + half_in], axis=1)

    def settle(s, total):
        t = s % 2
        if s < 2:
            value, slope = gelu_parts(total)
            slope_ref[t] = slope
            wide[0, t, z] = value.astype(BF)
        else:
            wide[1, t, z] = (total * slope_ref[t]).astype(BF)

    def rs_chain(s, i):
        if i == 0:
            rs_first(s, 0)
        elif i < hz:
            rs_wait(s, i - 1)
            for way in range(2):
                value = part[s, chunk_at(signs[way] * (hz - i))]
                if i == 1:
                    value = with_half(s, way, value)
                else:
                    value = value + z_recv[s, way, i - 1].astype(F32)
                z_send[s, way, i] = value.astype(BF)
                rs_send(s, i, way, 0)
        else:
            rs_wait(s, hz - 1)
            settle(s, part[s, z] + (z_recv[s, 0, hz - 1].astype(F32) + z_recv[s, 1, hz - 1].astype(F32)))

    def rs_short(s, i):
        if i == 0:
            for way in range(2):
                z_send[s, way, 1] = part[s, chunk_at(signs[way] * 3)].astype(BF)
                rs_send(s, 1, way, 0)
            rs_first(s, 1)
            for way in range(2):
                z_send[s, way, 2] = part[s, chunk_at(signs[way])].astype(BF)
                rs_send(s, 2, way, 0)
        elif i == 1:
            rs_wait(s, 1)
            rs_wait(s, 0)
            for way in range(2):
                value = part[s, chunk_at(signs[way] * 2)] + z_recv[s, way, 1].astype(F32)
                z_send[s, way, 3] = with_half(s, way, value).astype(BF)
                rs_send(s, 3, way, 1)
        else:
            rs_wait(s, 2)
            rs_wait(s, 3)
            total = part[s, z]
            for k in (2, 3):
                total = total + (z_recv[s, 0, k].astype(F32) + z_recv[s, 1, k].astype(F32))
            settle(s, total)

    def ag_block(s, way, i):
        block = (s // 2, s % 2, chunk_at(-signs[way] * i))
        return block + (pl.ds(16 * way, 16),) if i == hz else block

    def ag_send(s, way, i, far):
        block = wide.at[ag_block(s, way, i - 1 - far) + ((pl.ds(16 * way, 16),) if i == hz else ())]
        launch(remote(block, block, send_sem.at[4], a_rsem.at[s, way, i - 1], hop[far][way]))

    def ag_wait(s, i):
        for way in range(2):
            arrived(wide.at[ag_block(s, way, i)], a_rsem.at[s, way, i - 1])

    def ag_chain(s, i):
        if i > 0:
            ag_wait(s, i)
        if i < hz:
            for way in range(2):
                ag_send(s, way, i + 1, 0)

    def ag_short(s, i):
        if i == 0:
            for way in range(2):
                ag_send(s, way, 2, 1)
            for way in range(2):
                ag_send(s, way, 1, 0)
        elif i == 1:
            ag_wait(s, 2)
            for way in range(2):
                ag_send(s, way, 3, 0)
            for way in range(2):
                ag_send(s, way, 4, 1)
        else:
            for k in (1, 3, 4):
                ag_wait(s, k)

    def rs_step(s, i):
        (rs_short if s in SHORT_SUMS else rs_chain)(s, i)

    def ag_step(s, i):
        (ag_short if s in SHORT_GATHERS else ag_chain)(s, i)

    def product(s, early):
        a, t = s // 2, s % 2
        near = hz - 2
        if early is None:
            chunks = list(range(nz))
        else:
            chunks = [chunk_at(d) for d in (range(-near, near + 1) if early else range(near + 1, nz - near))]
        rows = jnp.concatenate([wide[a, t, k] for k in chunks], axis=0)
        each = rows.shape[0] // len(chunks)
        per = each // 16
        for which, ref in ((o, oth_sum), (c, own_sum)):
            step = 256 if half % 256 == 0 else half
            for k in range(0, half, step):
                if a == 0:
                    value = contract(rows, wout[which, :, k:k + step], 1, 0)
                else:
                    value = contract(rows, win[which, k:k + step, :], 1, 1)
                for i, chunk in enumerate(chunks):
                    ref[s, pl.ds(chunk * per, per), :, k:k + step] = value[i * each:(i + 1) * each].reshape(per, 16, step)
            if ref is oth_sum:
                for chunk in chunks:
                    there = pl.ds(chunk * per, per)
                    launch(remote(
                        oth_sum.at[s, there], sib_sum.at[s, there], send_sem.at[7 + s], sib_rsem.at[s], sibling
                    ))

    def spread(s):
        arrived(sib_sum.at[s], sib_rsem.at[s])
        for e in (2, 1, 3, 0):
            for d in (2, 1, 3, 0):
                if (d, e) == (0, 0) or d >= n or e >= n:
                    continue
                b = ahead(y, e) * n + ahead(x, d)
                k = e * n + d - 1
                out_send[s, k] = (own_sum[s, b] + sib_sum[s, b]).astype(BF)
                launch(remote(out_send.at[s, k], out_recv.at[s, k], send_sem.at[5], out_rsem.at[s], at(x + d, y + e, z, c)))

    results = (out_ref, gin_ref)

    def finish(s):
        a, t = s // 2, s % 2
        value = own_sum[s, y * n + x] + sib_sum[s, y * n + x]
        arrived(out_recv.at[s], out_rsem.at[s])
        for k in range(n * n - 1):
            value = value + out_recv[s, k].astype(F32)
        value = value.astype(BF)

        @pl.when(c != t)
        def _():
            fin_send[a] = value
            remote(fin_send.at[a], fin_recv.at[a], send_sem.at[6], fin_rsem.at[a], sibling).start()

        @pl.when(c == t)
        def _():
            cols = slice(t * half, (t + 1) * half)
            results[a][:, cols] = value

    def collect(a):
        arrived(fin_recv.at[a], fin_rsem.at[a])
        for t in range(2):
            @pl.when(c == t)
            def _():
                cols = slice((1 - t) * half, (2 - t) * half)
                results[a][:, cols] = fin_recv[a]

    def grad_w_out(h):
        cols = jnp.concatenate([rows_of(1, h, t) for t in range(2)], axis=0)
        step = 256 if width % 256 == 0 else width
        for k in range(0, width, step):
            left_rows = wide[0, :, :, :, k:k + step].reshape(-1, step)
            gw_out[h, k:k + step, :] = (contract(left_rows, cols, 0, 0) * factor).astype(BF)

    def grad_w_in(h):
        cols = wide[1].reshape(-1, width)
        step = 256 if half % 256 == 0 else half
        rows = jnp.concatenate([rows_of(0, h, t) for t in range(2)], axis=0)
        for k in range(0, half, step):
            gw_in[h, k:k + step, :] = (contract(rows[:, k:k + step], cols, 0, 0) * factor).astype(BF)

    def weights(a):
        arrived((win, wout)[a], w_sem.at[a])

    steps = {
        "s1": s1, "s2": s2, "s3": s3, "s4": s4, "weights": weights, "partial": partial, "rs_step": rs_step, "ag_step": ag_step,
        "product": product, "spread": spread, "finish": finish, "collect": collect, "drain": drain,
        "grad_w_out": grad_w_out, "grad_w_in": grad_w_in,
    }
    for step, *place in SCHEDULE:
        steps[step](*place)


def hand_over(out, gin, gw_in, gw_out, out_to, gin_to, gw_in_to, gw_out_to, sem):
    half = gw_in.shape[1]
    parts = 4
    step = half // parts
    copies = []
    for h in range(2):
        for p in range(parts):
            k = len(copies)
            copies.append(pltpu.make_async_copy(
                gw_in.at[h, pl.ds(p * step, step)], gw_in_to.at[pl.ds(h * half + p * step, step), :], sem.at[k]
            ))
            copies.append(pltpu.make_async_copy(
                gw_out.at[h, pl.ds(p * step, step)], gw_out_to.at[pl.ds(p * step, step), pl.ds(h * half, half)], sem.at[k + 1]
            ))
    copies.append(pltpu.make_async_copy(out, out_to, sem.at[len(copies)]))
    copies.append(pltpu.make_async_copy(gin, gin_to, sem.at[len(copies)]))
    for copy in copies:
        copy.start()
    for copy in copies:
        copy.wait()


def shards(n, nz, inputs, w_in, w_out, grad_out):
    rows, wide_cols = inputs.shape
    half = wide_cols // 2
    quarter = half // 2
    width = w_in.shape[1]
    tokens = 2 * n * n * rows
    chunk = n * n * rows // nz
    any_spec = pl.BlockSpec(memory_space=pl.ANY)
    vmem_spec = pl.BlockSpec(memory_space=pltpu.VMEM)
    dma = pltpu.SemaphoreType.DMA
    hz = nz // 2
    scratch = [
        pltpu.VMEM((2, 2, 2, 2, n, n, rows, quarter), BF),
        pltpu.VMEM((2, half, width), BF),
        pltpu.VMEM((2, width, half), BF),
        pltpu.VMEM((4, nz, chunk, width), F32),
        pltpu.VMEM((4, 2, hz, chunk, width), BF),
        pltpu.VMEM((4, 2, hz, chunk, width), BF),
        pltpu.VMEM((2, chunk, width), F32),
        pltpu.VMEM((2, 2, nz, chunk, width), BF),
        pltpu.VMEM((4, n * n, rows, half), F32),
        pltpu.VMEM((4, n * n, rows, half), F32),
        pltpu.VMEM((4, n * n, rows, half), F32),
        pltpu.VMEM((4, n * n - 1, rows, half), BF),
        pltpu.VMEM((4, n * n - 1, rows, half), BF),
        pltpu.VMEM((2, rows, half), BF),
        pltpu.VMEM((2, rows, half), BF),
        pltpu.VMEM((2, 2, 2, rows, quarter), BF),
        dma((2,)), dma((2,)), dma((2, 2, 2)), dma((2, 2, 2, n - 1)), dma((2, 2)), dma((4, hz)), dma((4, 2, hz)),
        dma((4,)), dma((4,)), dma((2,)), dma((11,)),
    ]
    results = pl.pallas_call(
        functools.partial(body, n, nz, 1.0 / tokens ** 0.5),
        name="ffn",
        out_shape=(
            pltpu.VMEM(inputs.shape, BF),
            pltpu.VMEM(inputs.shape, BF),
            pltpu.VMEM((2, half, width), BF),
            pltpu.VMEM((2, width, half), BF),
        ),
        in_specs=[any_spec] * 4,
        out_specs=(vmem_spec,) * 4,
        scratch_shapes=scratch,
        compiler_params=pltpu.CompilerParams(
            collective_id=0, has_side_effects=True, vmem_limit_bytes=48 * 2 ** 20
        ),
        cost_estimate=pl.CostEstimate(
            flops=12 * tokens * wide_cols * width, bytes_accessed=8 * wide_cols * width, transcendentals=0
        ),
    )(*(pltpu.with_memory_space_constraint(r, pltpu.HBM) for r in (inputs, w_in, w_out, grad_out)))
    return pl.pallas_call(
        hand_over,
        name="hand_over",
        out_shape=tuple(jax.ShapeDtypeStruct(a.shape, BF) for a in (inputs, inputs, w_in, w_out)),
        in_specs=[vmem_spec] * 4,
        out_specs=[any_spec] * 4,
        scratch_shapes=[dma((18,))],
        compiler_params=pltpu.CompilerParams(vmem_limit_bytes=4 * 2 ** 20),
    )(*(pltpu.with_memory_space_constraint(r, pltpu.VMEM) for r in results))


def solution(mesh):
    n, nz = mesh.shape["row"], mesh.shape["col"]
    in_specs = (
        P(("row", "depth"), "col"),
        P("col", ("row", "depth")),
        P(("row", "depth"), "col"),
        P(("row", "depth"), "col"),
    )
    out_specs = (
        P(("row", "depth"), "col"),
        P(("row", "depth"), "col"),
        P("col", ("row", "depth")),
        P(("row", "depth"), "col"),
    )
    return jax.shard_map(
        functools.partial(shards, n, nz), mesh=mesh, in_specs=in_specs, out_specs=out_specs, check_vma=False
    )
```

time: 415 us -> 78.3 us (0.19)
  waiting for transfers between devices: 325 us -> 0 us
  Pallas kernels: 0 us -> 77.6 us
  blocking collectives: 39.8 us -> 0 us
  matrix products: 25.3 us -> 0 us
  between operations: 14.1 us -> 0.64 us
  local copies, waits for them, and re-layouts: 5.19 us -> 0 us
  other arithmetic: 4.19 us -> 0 us
    reduce_scatter x4 -> x0, waiting for transfers between devices: 223 us -> none  [the longest x2 147 us: width_side(): lax.psum_scatter(contract(left, weight, 1, weight_dim), ('row', 'depth'),...]
    all_gather x2 -> x0, waiting for transfers between devices: 101 us -> none  [the longest x1 54.4 us: shards(): lax.all_gather(grad_out, ('row', 'depth'), axis=0, tiled=True)]
    pallas_call x0 -> x2, Pallas kernels: none -> 77.6 us  [the longest x1 75.2 us: shards(): pl.pallas_call(functools.partial(body, n, nz, 1.0 / tokens ** 0.5), name=...]
    all_gather x2 -> x0, blocking collectives: 39.8 us -> none  [spread_rows(): return lax.all_gather(local, 'col', axis=0, tiled=True)]
    dot_general x6 -> x0, matrix products: 25.3 us -> none  [contract(): lax.dot_general(left, right, (((left_dim,), (right_dim,)), ((), ())), pre...]
    unnamed x5 -> x0, local copies, waits for them, and re-layouts: 5.19 us -> none
    convert_element_type x3 -> x0, other arithmetic: 4.19 us -> none  [the longest x1 1.52 us: shards(): outputs = width_side(act_rows, w_out, 0).astype(jnp.bfloat16)]
  transfers between devices with their start and end apart: 6 -> 0, of which waited for: 6 -> 0; matrix products, arithmetic and copies ran while one was open for 7% -> 0% of each run, Pallas kernels for 0% -> 0%
where the time goes in v2:
time: 78.3 us; the launch traced here: 78.2 us
  Pallas kernels  77.6 us (99%)
    pallas_call x1, Pallas kernels, shards(): pl.pallas_call(functools.partial(body, n, nz, 1.0 / tokens ** 0.5), name=...  75.2 us
    pallas_call x1, Pallas kernels, shards(): pl.pallas_call(hand_over, name='hand_over', out_shape=tuple((jax.ShapeDty...  2.34 us

profile of v2, /device:TPU:1, one launch (start us, length us, event | category | flops | bytes accessed | tf_op | source)
XLA Modules:
  0.0 78.2 jit_solution(4579781025163287175)
XLA Ops:
  0.6 75.2 %ffn.1 = (bf16[16,1536]{1,0:T(8,128)(2,1)S(1)}, bf16[16,1536]{1,0:T(8,128)(2,1)S(1)}, bf16[2,768,768]{2,1,0:T(8,128)(2,1)S(1)}, bf16[2,768,768]{2,1,0:T(8,128)(2,1)S(1)}) custom-call(bf16[16,1536]{1,0:T(8,128)(2,1)} %x_hbm.1, bf16[1536,768]{1,0:T(8,128)(2,1)} %win_hbm.1, bf16[768,1536]{1,0:T(8,128)(2,1)} %wout_hbm.1, bf16[16,1536]{1,0:T(8,128)(2,1)} %g_hbm.1), custom_call_target="tpu_custom_call" | custom-call | flops 7247757312 | bytes 9437184 | tf_op jit(solution)/shard_map/ffn/pallas_call | solution.py:459
  75.9 2.3 %hand_over.1 = (bf16[16,1536]{1,0:T(8,128)(2,1)}, bf16[16,1536]{1,0:T(8,128)(2,1)}, bf16[1536,768]{1,0:T(8,128)(2,1)}, bf16[768,1536]{1,0:T(8,128)(2,1)}) custom-call(bf16[16,1536]{1,0:T(8,128)(2,1)S(1)} %get-tuple-element.8.out, bf16[16,1536]{1,0:T(8,128)(2,1)S(1)} %get-tuple-element.9.gin, bf16[2,768,768]{2,1,0:T(8,128)(2,1)S(1)} %get-tuple-element.10.gw_in, ...), custom_call_target="tpu_custom_call" | custom-call | tf_op jit(solution)/shard_map/hand_over/pallas_call | solution.py:478

commit v3 on v2

--- a/solution.py
+++ b/solution.py
@@ -16,20 +16,22 @@
 SHORT_GATHERS = ()
 
 SCHEDULE = (
-    ("s1", 0), ("s1", 1), ("s2", 0, 1), ("s2", 0, 0), ("s2", 1, 0), ("s2", 1, 1), ("s3", 0, 1), ("s4", 0, 1),
-    ("weights", 0), ("partial", 0, 1), ("s3", 0, 0), ("rs_step", 1, 0), ("s4", 0, 0), ("partial", 0, 0),
-    ("rs_step", 0, 0), ("s3", 1, 0), ("rs_step", 1, 1), ("s3", 1, 1), ("s4", 1, 0), ("weights", 1), ("partial", 1, 0),
-    ("rs_step", 2, 0), ("s4", 1, 1), ("partial", 1, 1), ("rs_step", 3, 0), ("rs_step", 0, 1), ("rs_step", 1, 2),
-    ("rs_step", 2, 1), ("rs_step", 3, 1), ("rs_step", 0, 2), ("ag_step", 0, 0), ("rs_step", 1, 3), ("rs_step", 2, 2),
-    ("rs_step", 3, 2), ("ag_step", 0, 1), ("rs_step", 1, 4), ("ag_step", 1, 0), ("rs_step", 2, 3), ("rs_step", 3, 3),
-    ("ag_step", 0, 2), ("ag_step", 1, 1), ("rs_step", 2, 4), ("ag_step", 2, 0), ("rs_step", 3, 4), ("ag_step", 3, 0),
-    ("ag_step", 0, 3), ("product", 0, True), ("ag_step", 1, 2), ("ag_step", 2, 1), ("ag_step", 3, 1),
-    ("ag_step", 0, 4), ("product", 0, False), ("ag_step", 1, 3), ("product", 1, True), ("spread", 0),
-    ("ag_step", 3, 2), ("ag_step", 2, 2), ("ag_step", 1, 4), ("grad_w_out", 1), ("product", 1, False),
-    ("grad_w_out", 0), ("ag_step", 3, 3), ("product", 3, True), ("spread", 1), ("ag_step", 2, 3),
-    ("product", 2, True), ("finish", 0), ("ag_step", 3, 4), ("product", 3, False), ("ag_step", 2, 4),
-    ("product", 2, False), ("spread", 3), ("grad_w_in", 1), ("spread", 2), ("finish", 1), ("grad_w_in", 0),
-    ("collect", 0), ("finish", 3), ("finish", 2), ("collect", 1), ("drain",),
+    ("s1", 0), ("s1", 1), ("s2", 0, 1), ("s2", 0, 0), ("s2", 1, 1), ("s2", 1, 0), ("s3", 0, 1), ("weights", 0),
+    ("partial", 0, 1, False), ("s4", 0, 1), ("partial", 0, 1, True), ("s3", 0, 0), ("partial", 0, 0, False),
+    ("rs_step", 1, 0), ("s4", 0, 0), ("partial", 0, 0, True), ("rs_step", 0, 0), ("s3", 1, 1), ("weights", 1),
+    ("partial", 1, 1, False), ("s4", 1, 1), ("rs_step", 1, 1), ("s3", 1, 0), ("partial", 1, 0, False),
+    ("partial", 1, 1, True), ("s4", 1, 0), ("partial", 1, 0, True), ("rs_step", 2, 0), ("rs_step", 3, 0),
+    ("rs_step", 0, 1), ("rs_step", 1, 2), ("rs_step", 2, 1), ("rs_step", 3, 1), ("rs_step", 0, 2), ("ag_step", 0, 0),
+    ("rs_step", 1, 3), ("rs_step", 2, 2), ("rs_step", 3, 2), ("ag_step", 0, 1), ("rs_step", 1, 4), ("ag_step", 1, 0),
+    ("rs_step", 2, 3), ("rs_step", 3, 3), ("ag_step", 0, 2), ("ag_step", 1, 1), ("rs_step", 2, 4), ("ag_step", 2, 0),
+    ("rs_step", 3, 4), ("ag_step", 3, 0), ("ag_step", 0, 3), ("product", 0, True), ("ag_step", 1, 2),
+    ("ag_step", 2, 1), ("spread", 0, True), ("ag_step", 3, 1), ("ag_step", 0, 4), ("product", 0, False),
+    ("ag_step", 1, 3), ("product", 1, True), ("ag_step", 2, 2), ("spread", 0, False), ("ag_step", 3, 2),
+    ("spread", 1, True), ("ag_step", 1, 4), ("product", 1, False), ("grad_w_out", 0), ("ag_step", 2, 3),
+    ("product", 2, True), ("spread", 1, False), ("ag_step", 3, 3), ("finish", 0), ("product", 3, True),
+    ("spread", 2, True), ("ag_step", 2, 4), ("product", 2, False), ("spread", 3, True), ("ag_step", 3, 4),
+    ("grad_w_in", 0), ("product", 3, False), ("spread", 2, False), ("finish", 1), ("grad_w_in", 1), ("collect", 0),
+    ("grad_w_out", 1), ("spread", 3, False), ("finish", 2), ("finish", 3), ("collect", 1), ("drain",),
 )
 
 
@@ -99,7 +101,7 @@
     for h in range(2):
         w_copies.append(pltpu.make_async_copy(win_hbm.at[pl.ds(h * half, half), :], win.at[h], w_sem.at[0]))
         w_copies.append(pltpu.make_async_copy(wout_hbm.at[:, pl.ds(h * half, half)], wout.at[h], w_sem.at[1]))
-    for copy in x_copies + w_copies:
+    for copy in x_copies:
         copy.start()
 
     barrier = pltpu.get_barrier_semaphore()
@@ -157,6 +159,9 @@
             launch(pltpu.make_async_copy(
                 own_rows.at[a, c, q], acts.at[a, c, q, c, second, first], s1_rsem.at[a, c, q]
             ))
+        if a == 0:
+            for copy in w_copies:
+                copy.start()
 
     def s2(a, t):
         for q in range(2):
@@ -184,16 +189,20 @@
         across.append(jnp.concatenate([acts[a, h, 1, t, i, j] for j in range(n) for i in range(n)], axis=0))
         return jnp.concatenate(across, axis=1)
 
-    def partial(a, t):
+    def partial(a, t, theirs):
         s = 2 * a + t
-        rows = [rows_of(a, h, t) for h in range(2)]
+        h = o if theirs else c
+        rows = rows_of(a, h, t)
         step = 256 if width % 256 == 0 else width
         for k in range(0, width, step):
             if a == 0:
-                value = sum(contract(rows[h], win[h, :, k:k + step], 1, 0) for h in range(2))
+                value = contract(rows, win[h, :, k:k + step], 1, 0)
             else:
-                value = sum(contract(rows[h], wout[h, k:k + step, :], 1, 1) for h in range(2))
-            part[s, :, :, k:k + step] = value.reshape(nz, -1, step)
+                value = contract(rows, wout[h, k:k + step, :], 1, 1)
+            value = value.reshape(nz, -1, step)
+            if theirs:
+                value = value + part[s, :, :, k:k + step]
+            part[s, :, :, k:k + step] = value
 
     hz = nz // 2
     signs = (1, -1)
@@ -277,11 +286,12 @@
 
     def ag_send(s, way, i, far):
         block = wide.at[ag_block(s, way, i - 1 - far) + ((pl.ds(16 * way, 16),) if i == hz else ())]
-        launch(remote(block, block, send_sem.at[4], a_rsem.at[s, way, i - 1], hop[far][way]))
+        launch(remote(block, block, send_sem.at[4], a_rsem.at[s, i - 1], hop[far][way]))
 
     def ag_wait(s, i):
-        for way in range(2):
-            arrived(wide.at[ag_block(s, way, i)], a_rsem.at[s, way, i - 1])
+        a, t = s // 2, s % 2
+        both = wide.at[a, t, pl.ds(0, 2)] if i < hz else wide.at[a, t, 0]
+        arrived(both, a_rsem.at[s, i - 1])
 
     def ag_chain(s, i):
         if i > 0:
@@ -312,16 +322,17 @@
     def ag_step(s, i):
         (ag_short if s in SHORT_GATHERS else ag_chain)(s, i)
 
+    near = hz - 2
+
+    def span(early):
+        return (-near, 2 * near + 1) if early else (near + 1, nz - 2 * near - 1)
+
     def product(s, early):
         a, t = s // 2, s % 2
-        near = hz - 2
-        if early is None:
-            chunks = list(range(nz))
-        else:
-            chunks = [chunk_at(d) for d in (range(-near, near + 1) if early else range(near + 1, nz - near))]
+        low, count = span(early)
+        chunks = [chunk_at(low + d) for d in range(count)]
         rows = jnp.concatenate([wide[a, t, k] for k in chunks], axis=0)
         each = rows.shape[0] // len(chunks)
-        per = each // 16
         for which, ref in ((o, oth_sum), (c, own_sum)):
             step = 256 if half % 256 == 0 else half
             for k in range(0, half, step):
@@ -335,27 +346,35 @@
                 for chunk in chunks:
                     there = pl.ds(chunk * per, per)
                     launch(remote(
-                        oth_sum.at[s, there], sib_sum.at[s, there], send_sem.at[7 + s], sib_rsem.at[s], sibling
+                        oth_sum.at[s, there], sib_sum.at[s, there], send_sem.at[7 + s], sib_rsem.at[s, 0 if early else 1], sibling
                     ))
 
-    def spread(s):
-        arrived(sib_sum.at[s], sib_rsem.at[s])
-        for e in (2, 1, 3, 0):
-            for d in (2, 1, 3, 0):
-                if (d, e) == (0, 0) or d >= n or e >= n:
-                    continue
-                b = ahead(y, e) * n + ahead(x, d)
-                k = e * n + d - 1
-                out_send[s, k] = (own_sum[s, b] + sib_sum[s, b]).astype(BF)
-                launch(remote(out_send.at[s, k], out_recv.at[s, k], send_sem.at[5], out_rsem.at[s], at(x + d, y + e, z, c)))
+    mine = y * n + x
+    per = n * n // nz
+
+    def spread(s, early):
+        low, count = span(early)
+        count = count * per
+        arrived(sib_sum.at[s, pl.ds(0, count)], sib_rsem.at[s, 0 if early else 1])
+        for i in range(count):
+            k = lax.rem(mine + i, count)
+            b = chunk_at(low + k // per) * per + lax.rem(k, per)
+
+            @pl.when(b != mine)
+            def _():
+                out_send[s, b] = (own_sum[s, b] + sib_sum[s, b]).astype(BF)
+                remote(
+                    out_send.at[s, b], out_recv.at[s, mine], send_sem.at[5], out_rsem.at[s], at(lax.rem(b, n), b // n, z, c)
+                ).start()
 
     results = (out_ref, gin_ref)
 
     def finish(s):
         a, t = s // 2, s % 2
-        value = own_sum[s, y * n + x] + sib_sum[s, y * n + x]
-        arrived(out_recv.at[s], out_rsem.at[s])
-        for k in range(n * n - 1):
+        out_recv[s, mine] = jnp.zeros(out_recv.shape[2:], BF)
+        value = own_sum[s, mine] + sib_sum[s, mine]
+        arrived(out_recv.at[s, pl.ds(0, n * n - 1)], out_rsem.at[s])
+        for k in range(n * n):
             value = value + out_recv[s, k].astype(F32)
         value = value.astype(BF)
 
@@ -448,13 +467,13 @@
         pltpu.VMEM((4, n * n, rows, half), F32),
         pltpu.VMEM((4, n * n, rows, half), F32),
         pltpu.VMEM((4, n * n, rows, half), F32),
-        pltpu.VMEM((4, n * n - 1, rows, half), BF),
-        pltpu.VMEM((4, n * n - 1, rows, half), BF),
+        pltpu.VMEM((4, n * n, rows, half), BF),
+        pltpu.VMEM((4, n * n, rows, half), BF),
         pltpu.VMEM((2, rows, half), BF),
         pltpu.VMEM((2, rows, half), BF),
         pltpu.VMEM((2, 2, 2, rows, quarter), BF),
-        dma((2,)), dma((2,)), dma((2, 2, 2)), dma((2, 2, 2, n - 1)), dma((2, 2)), dma((4, hz)), dma((4, 2, hz)),
-        dma((4,)), dma((4,)), dma((2,)), dma((11,)),
+        dma((2,)), dma((2,)), dma((2, 2, 2)), dma((2, 2, 2, n - 1)), dma((2, 2)), dma((4, hz)), dma((4, hz)),
+        dma((4, 2)), dma((4,)), dma((2,)), dma((11,)),
     ]
     results = pl.pallas_call(
         functools.partial(body, n, nz, 1.0 / tokens ** 0.5),

time: 78.3 us -> 76.9 us (0.982)
  the two profiles are of different devices: /device:TPU:1 before, /device:TPU:17 now
where the time goes in v3:
time: 76.9 us; the launch traced here: 76.8 us
  Pallas kernels  76.1 us (99%)
    pallas_call x1, Pallas kernels, shards(): pl.pallas_call(functools.partial(body, n, nz, 1.0 / tokens ** 0.5), name=...  73.8 us
    pallas_call x1, Pallas kernels, shards(): pl.pallas_call(hand_over, name='hand_over', out_shape=tuple((jax.ShapeDty...  2.34 us

profile of v3, /device:TPU:17, one launch (start us, length us, event | category | flops | bytes accessed | tf_op | source)
XLA Modules:
  0.0 76.8 jit_solution(2594756521801510954)
XLA Ops:
  0.6 73.8 %ffn.1 = (bf16[16,1536]{1,0:T(8,128)(2,1)S(1)}, bf16[16,1536]{1,0:T(8,128)(2,1)S(1)}, bf16[2,768,768]{2,1,0:T(8,128)(2,1)S(1)}, bf16[2,768,768]{2,1,0:T(8,128)(2,1)S(1)}) custom-call(bf16[16,1536]{1,0:T(8,128)(2,1)} %x_hbm.1, bf16[1536,768]{1,0:T(8,128)(2,1)} %win_hbm.1, bf16[768,1536]{1,0:T(8,128)(2,1)} %wout_hbm.1, bf16[16,1536]{1,0:T(8,128)(2,1)} %g_hbm.1), custom_call_target="tpu_custom_call" | custom-call | flops 7247757312 | bytes 9437184 | tf_op jit(solution)/shard_map/ffn/pallas_call | solution.py:478
  74.4 2.3 %hand_over.1 = (bf16[16,1536]{1,0:T(8,128)(2,1)}, bf16[16,1536]{1,0:T(8,128)(2,1)}, bf16[1536,768]{1,0:T(8,128)(2,1)}, bf16[768,1536]{1,0:T(8,128)(2,1)}) custom-call(bf16[16,1536]{1,0:T(8,128)(2,1)S(1)} %get-tuple-element.8.out, bf16[16,1536]{1,0:T(8,128)(2,1)S(1)} %get-tuple-element.9.gin, bf16[2,768,768]{2,1,0:T(8,128)(2,1)S(1)} %get-tuple-element.10.gw_in, ...), custom_call_target="tpu_custom_call" | custom-call | tf_op jit(solution)/shard_map/hand_over/pallas_call | solution.py:497

commit v4 on v3

--- a/solution.py
+++ b/solution.py
@@ -17,21 +17,22 @@
 
 SCHEDULE = (
     ("s1", 0), ("s1", 1), ("s2", 0, 1), ("s2", 0, 0), ("s2", 1, 1), ("s2", 1, 0), ("s3", 0, 1), ("weights", 0),
-    ("partial", 0, 1, False), ("s4", 0, 1), ("partial", 0, 1, True), ("s3", 0, 0), ("partial", 0, 0, False),
-    ("rs_step", 1, 0), ("s4", 0, 0), ("partial", 0, 0, True), ("rs_step", 0, 0), ("s3", 1, 1), ("weights", 1),
-    ("partial", 1, 1, False), ("s4", 1, 1), ("rs_step", 1, 1), ("s3", 1, 0), ("partial", 1, 0, False),
-    ("partial", 1, 1, True), ("s4", 1, 0), ("partial", 1, 0, True), ("rs_step", 2, 0), ("rs_step", 3, 0),
-    ("rs_step", 0, 1), ("rs_step", 1, 2), ("rs_step", 2, 1), ("rs_step", 3, 1), ("rs_step", 0, 2), ("ag_step", 0, 0),
-    ("rs_step", 1, 3), ("rs_step", 2, 2), ("rs_step", 3, 2), ("ag_step", 0, 1), ("rs_step", 1, 4), ("ag_step", 1, 0),
-    ("rs_step", 2, 3), ("rs_step", 3, 3), ("ag_step", 0, 2), ("ag_step", 1, 1), ("rs_step", 2, 4), ("ag_step", 2, 0),
-    ("rs_step", 3, 4), ("ag_step", 3, 0), ("ag_step", 0, 3), ("product", 0, True), ("ag_step", 1, 2),
-    ("ag_step", 2, 1), ("spread", 0, True), ("ag_step", 3, 1), ("ag_step", 0, 4), ("product", 0, False),
-    ("ag_step", 1, 3), ("product", 1, True), ("ag_step", 2, 2), ("spread", 0, False), ("ag_step", 3, 2),
-    ("spread", 1, True), ("ag_step", 1, 4), ("product", 1, False), ("grad_w_out", 0), ("ag_step", 2, 3),
-    ("product", 2, True), ("spread", 1, False), ("ag_step", 3, 3), ("finish", 0), ("product", 3, True),
-    ("spread", 2, True), ("ag_step", 2, 4), ("product", 2, False), ("spread", 3, True), ("ag_step", 3, 4),
-    ("grad_w_in", 0), ("product", 3, False), ("spread", 2, False), ("finish", 1), ("grad_w_in", 1), ("collect", 0),
-    ("grad_w_out", 1), ("spread", 3, False), ("finish", 2), ("finish", 3), ("collect", 1), ("drain",),
+    ("partial", 0, 1, False), ("s4", 0, 1), ("partial", 0, 1, True), ("s3", 0, 0), ("rs_step", 1, 0),
+    ("partial", 0, 0, False), ("s4", 0, 0), ("partial", 0, 0, True), ("rs_step", 0, 0), ("s3", 1, 1), ("weights", 1),
+    ("partial", 1, 1, False), ("rs_step", 1, 1), ("s4", 1, 1), ("partial", 1, 1, True), ("rs_step", 3, 0),
+    ("s3", 1, 0), ("partial", 1, 0, False), ("s4", 1, 0), ("partial", 1, 0, True), ("rs_step", 2, 0),
+    ("rs_step", 0, 1), ("rs_step", 1, 2), ("rs_step", 3, 1), ("rs_step", 2, 1), ("rs_step", 0, 2), ("ag_step", 0, 0),
+    ("rs_step", 1, 3), ("rs_step", 3, 2), ("rs_step", 2, 2), ("ag_step", 0, 1), ("rs_step", 1, 4), ("ag_step", 1, 0),
+    ("rs_step", 3, 3), ("rs_step", 2, 3), ("ag_step", 0, 2), ("product", 0, True), ("ag_step", 1, 1),
+    ("rs_step", 3, 4), ("ag_step", 3, 0), ("spread", 0, True), ("rs_step", 2, 4), ("ag_step", 2, 0),
+    ("ag_step", 0, 3), ("ag_step", 1, 2), ("product", 1, True), ("ag_step", 3, 1), ("ag_step", 2, 1),
+    ("spread", 1, True), ("ag_step", 0, 4), ("product", 0, False), ("ag_step", 1, 3), ("ag_step", 3, 2),
+    ("product", 3, True), ("spread", 0, False), ("ag_step", 2, 2), ("product", 2, True), ("ag_step", 1, 4),
+    ("product", 1, False), ("spread", 3, True), ("grad_w_out", 0), ("ag_step", 3, 3), ("spread", 1, False),
+    ("ag_step", 2, 3), ("spread", 2, True), ("finish", 0), ("grad_w_out", 1), ("ag_step", 3, 4),
+    ("product", 3, False), ("ag_step", 2, 4), ("product", 2, False), ("grad_w_in", 0), ("spread", 3, False),
+    ("spread", 2, False), ("finish", 1), ("grad_w_in", 1), ("collect", 0), ("finish", 3), ("finish", 2),
+    ("collect", 1), ("drain",),
 )
 
 

time: 76.9 us -> 75.6 us (0.983)
  the two profiles are of different devices: /device:TPU:17 before, /device:TPU:15 now
where the time goes in v4:
time: 75.6 us; the launch traced here: 75.5 us
  Pallas kernels  74.9 us (99%)
    pallas_call x1, Pallas kernels, shards(): pl.pallas_call(functools.partial(body, n, nz, 1.0 / tokens ** 0.5), name=...  72.5 us
    pallas_call x1, Pallas kernels, shards(): pl.pallas_call(hand_over, name='hand_over', out_shape=tuple((jax.ShapeDty...  2.34 us

profile of v4, /device:TPU:15, one launch (start us, length us, event | category | flops | bytes accessed | tf_op | source)
XLA Modules:
  0.0 75.5 jit_solution(14079804094276394460)
XLA Ops:
  0.6 72.5 %ffn.1 = (bf16[16,1536]{1,0:T(8,128)(2,1)S(1)}, bf16[16,1536]{1,0:T(8,128)(2,1)S(1)}, bf16[2,768,768]{2,1,0:T(8,128)(2,1)S(1)}, bf16[2,768,768]{2,1,0:T(8,128)(2,1)S(1)}) custom-call(bf16[16,1536]{1,0:T(8,128)(2,1)} %x_hbm.1, bf16[1536,768]{1,0:T(8,128)(2,1)} %win_hbm.1, bf16[768,1536]{1,0:T(8,128)(2,1)} %wout_hbm.1, bf16[16,1536]{1,0:T(8,128)(2,1)} %g_hbm.1), custom_call_target="tpu_custom_call" | custom-call | flops 7247757312 | bytes 9437184 | tf_op jit(solution)/shard_map/ffn/pallas_call | solution.py:479
  73.2 2.3 %hand_over.1 = (bf16[16,1536]{1,0:T(8,128)(2,1)}, bf16[16,1536]{1,0:T(8,128)(2,1)}, bf16[1536,768]{1,0:T(8,128)(2,1)}, bf16[768,1536]{1,0:T(8,128)(2,1)}) custom-call(bf16[16,1536]{1,0:T(8,128)(2,1)S(1)} %get-tuple-element.8.out, bf16[16,1536]{1,0:T(8,128)(2,1)S(1)} %get-tuple-element.9.gin, bf16[2,768,768]{2,1,0:T(8,128)(2,1)S(1)} %get-tuple-element.10.gw_in, ...), custom_call_target="tpu_custom_call" | custom-call | tf_op jit(solution)/shard_map/hand_over/pallas_call | solution.py:498
